TPU v7x, 32 devices: a whole 2x2x4 slice. The times are simulated.
32 devices in a mesh: cx: 4 (over y, x), cy: 8 (over z, core).
Axes of the slice: x: 2, y: 2, z: 4, core: 2. Of those that a mesh axis runs over, the one named last changes fastest.
Arguments:
- query_rows: bfloat16 [8192, 1024], P(('cx', 'cy')), may hold values from -6 to 6
- key_rows: bfloat16 [8192, 1024], P(('cx', 'cy')), may hold values from -6 to 6
- value_rows: bfloat16 [8192, 1024], P(('cx', 'cy')), may hold values from -6 to 6
- forward_out: bfloat16 [8192, 1024], P(('cx', 'cy')), may hold values from -6 to 6
- out_grad: bfloat16 [8192, 1024], P(('cx', 'cy')), may hold values from -6 to 6
- doc_blocks: int32 [8], replicated, may hold values from 1 to 15, 64 in all
Outputs:
- query_grad: bfloat16 [8192, 1024], P(('cx', 'cy'))
- key_grad: bfloat16 [8192, 1024], P(('cx', 'cy'))
- value_grad: bfloat16 [8192, 1024], P(('cx', 'cy'))
Inputs may be any that keep to these rules, and one draw needn't show every extreme that they name: `doc_blocks`: lengths of the documents in blocks of 128 tokens, in sequence order, summing to 64; the longest has exactly 15 blocks.
All inputs are finite; a program needn't handle non-finite values.
Results may differ from a plain program's by a relative error of at most 0.0049.
Values may be sent and summed in bfloat16 or wider, within the bound.
A program may use at most 128 MiB of HBM per device.

v0:
```python
import math

import jax
import jax.numpy as jnp
from jax import lax
from jax.experimental import pallas as pl
from jax.experimental.pallas import tpu as pltpu
from jax.sharding import PartitionSpec as P

HEADS = 8
DH = 128
BLOCK = 128
REACH = 7
GROUP = 8
WIDE = 2
EXP2_SCALE = math.log2(math.e) / math.sqrt(DH)
MESH = pl.DeviceIdType.MESH
NT = (((1,), (1,)), ((), ()))
TN = (((0,), (0,)), ((), ()))


def place():
    inner = lax.axis_size("cy")
    count = lax.axis_size("cx") * inner
    shard = lax.axis_index("cx") * inner + lax.axis_index("cy")

    def device(index):
        return (index // inner, lax.rem(index, inner))

    return count, shard, device


def rows_at(index, rows):
    return pl.ds(pl.multiple_of(index * rows, rows), rows)


def cols_at(head):
    return pl.ds(pl.multiple_of(head * DH, DH), DH)


def spread_kernel(
    docs, q_ref, k_ref, v_ref, o_ref, g_ref, qh, gh, kw, vw, dh, lh,
    o_here, g_here, dsend, send, recv, fsend, frecv, local
):
    rows = q_ref.shape[0]
    count, shard, device = place()
    me = lax.rem(shard, GROUP)
    base = shard - me
    ahead = device(lax.rem(shard + GROUP, count))
    behind = device(lax.rem(shard + count - GROUP, count))
    tensors = ((k_ref, kw, REACH), (v_ref, vw, REACH), (q_ref, qh, 0), (g_ref, gh, 0))
    K, V, Q, G, DELTA = range(5)

    def out_copy(which, j):
        src, dst, shift = tensors[which]
        peer = lax.rem(me + j, GROUP)
        return pltpu.make_async_remote_copy(
            src_ref=src.at[:, cols_at(peer)],
            dst_ref=dst.at[rows_at(me + shift, rows), :],
            send_sem=send.at[which, j],
            recv_sem=recv.at[which, j],
            device_id=device(base + peer),
            device_id_type=MESH,
        )

    def in_copy(which, j):
        src, dst, shift = tensors[which]
        peer = lax.rem(me + GROUP - j, GROUP)
        return pltpu.make_async_remote_copy(
            src_ref=src.at[:, cols_at(peer)],
            dst_ref=dst.at[rows_at(peer + shift, rows), :],
            send_sem=send.at[which, j],
            recv_sem=recv.at[which, j],
            device_id=device(base + peer),
            device_id_type=MESH,
        )

    def own_copy(which):
        src, dst, shift = tensors[which]
        return pltpu.make_async_copy(
            src.at[:, cols_at(me)], dst.at[rows_at(me + shift, rows), :], local.at[which]
        )

    def forward(which, shard_in_group):
        _, dst, shift = tensors[which]
        return pltpu.make_async_remote_copy(
            src_ref=dst.at[rows_at(shard_in_group + shift, rows), :],
            dst_ref=dst.at[rows_at(shard_in_group - 1, rows), :],
            send_sem=fsend.at[which, shard_in_group],
            recv_sem=frecv.at[which, shard_in_group],
            device_id=ahead,
            device_id_type=MESH,
        )

    def forward_all(which):
        own_copy(which).wait()

        @pl.when(me >= 1)
        def _():
            forward(which, me).start()

        for j in range(1, GROUP):
            source = lax.rem(me + GROUP - j, GROUP)
            in_copy(which, j).wait_recv()

            @pl.when(source >= 1)
            def _():
                forward(which, source).start()

    g_copy = pltpu.make_async_copy(g_ref, g_here, local.at[5])
    o_copy = pltpu.make_async_copy(o_ref, o_here, local.at[6])
    barrier = pltpu.get_barrier_semaphore()
    for j in range(1, GROUP):
        peer = device(base + lax.rem(me + j, GROUP))
        pl.semaphore_signal(barrier, inc=1, device_id=peer, device_id_type=MESH)
    pl.semaphore_signal(barrier, inc=1, device_id=behind, device_id_type=MESH)
    for which in range(4):
        own_copy(which).start()
    g_copy.start()
    o_copy.start()
    pl.semaphore_wait(barrier, GROUP)

    for which in (K, Q):
        for j in range(1, GROUP):
            out_copy(which, j).start()

    g_copy.wait()
    o_copy.wait()
    ones = jnp.ones((8, DH), jnp.bfloat16)
    for head in range(HEADS):
        cols = slice(head * DH, (head + 1) * DH)
        product = g_here[:, cols].astype(jnp.float32) * o_here[:, cols].astype(jnp.float32)
        high = product.astype(jnp.bfloat16)
        low = (product - high.astype(jnp.float32)).astype(jnp.bfloat16)
        dsend[head] = lax.dot_general(
            ones, high, NT, preferred_element_type=jnp.float32
        ) + lax.dot_general(ones, low, NT, preferred_element_type=jnp.float32)

    def delta_copy(j, peer, source):
        return pltpu.make_async_remote_copy(
            src_ref=dsend.at[peer],
            dst_ref=dh.at[source],
            send_sem=send.at[DELTA, j],
            recv_sem=recv.at[DELTA, j],
            device_id=device(base + peer),
            device_id_type=MESH,
        )

    own_delta = pltpu.make_async_copy(dsend.at[me], dh.at[me], local.at[DELTA])
    own_delta.start()
    for j in range(1, GROUP):
        delta_copy(j, lax.rem(me + j, GROUP), me).start()

    forward_all(K)
    for which in (V, G):
        for j in range(1, GROUP):
            out_copy(which, j).start()
    own_copy(Q).wait()
    for j in range(1, GROUP):
        in_copy(Q, j).wait_recv()
    for s in range(1, GROUP):
        forward(K, s).wait_recv()

    masked = mask_maker(docs, base, rows)

    def stats(i, _):
        _, allowed = masked(i)
        q = qh[rows_at(i, rows), :]
        top = jnp.full((1, rows), -1e30, jnp.float32)
        total = jnp.zeros((1, rows), jnp.float32)
        for c in range((REACH + 1) // WIDE):
            j = i + c * WIDE
            s = lax.dot_general(
                kw[wide_at(j, rows), :], q, NT, preferred_element_type=jnp.float32
            )
            s = jnp.where(allowed(j), s * EXP2_SCALE, -1e30)
            higher = jnp.maximum(top, jnp.max(s, axis=0, keepdims=True))
            total = total * jnp.exp2(top - higher) + jnp.sum(
                jnp.exp2(s - higher), axis=0, keepdims=True
            )
            top = higher
        lh[i] = jnp.broadcast_to(top + jnp.log2(total), (8, rows))
        return 0

    lax.fori_loop(0, GROUP, stats, 0)
    forward_all(V)
    own_copy(G).wait()
    for j in range(1, GROUP):
        in_copy(G, j).wait_recv()
    own_delta.wait()
    for j in range(1, GROUP):
        peer = lax.rem(me + GROUP - j, GROUP)
        delta_copy(j, peer, peer).wait_recv()
    for s in range(1, GROUP):
        forward(V, s).wait_recv()
    for s in range(1, GROUP):
        for which in (K, V):
            forward(which, s).wait_send()
    for j in range(1, GROUP):
        for which in range(4):
            out_copy(which, j).wait_send()
        delta_copy(j, lax.rem(me + j, GROUP), me).wait_send()


def mask_maker(docs, base, rows):
    per_tile = rows // BLOCK
    group_block = base * per_tile
    key_at = lax.broadcasted_iota(jnp.int32, (WIDE * rows, rows), 0)
    lane = lax.broadcasted_iota(jnp.int32, (1, rows), 1)

    def masked(i):
        first_block = group_block + i * per_tile

        def look(n, state):
            start, firsts = state
            firsts = tuple(
                jnp.where(start <= first_block + b, start, firsts[b]) for b in range(per_tile)
            )
            return start + docs[n], firsts

        _, firsts = lax.fori_loop(
            0,
            docs.shape[0],
            look,
            (jnp.int32(0), tuple(jnp.int32(0) for _ in range(per_tile))),
        )
        firsts = [f - group_block + REACH * per_tile for f in firsts]
        start_row = jnp.full((1, rows), 0, jnp.int32)
        for b in range(per_tile):
            start_row = jnp.where(lane >= b * BLOCK, firsts[b] * BLOCK, start_row)
        last_row = (i + REACH) * rows + lane

        def allowed(j):
            return (key_at >= start_row - j * rows) & (key_at <= last_row - j * rows)

        return firsts[0] // per_tile, allowed

    return masked


def wide_at(j, rows):
    return pl.ds(pl.multiple_of(j * rows, rows), WIDE * rows)


def grad_kernel(
    docs, q_ref, g_ref, k_ref, v_ref, d_ref, l_ref, dq_ref, dk_ref, dv_ref, hk_ref, hv_ref, dk, dv
):
    rows = q_ref.shape[0] // GROUP
    scale = 1.0 / math.sqrt(DH)
    _, shard, _ = place()
    dk[...] = jnp.zeros_like(dk)
    dv[...] = jnp.zeros_like(dv)
    masked = mask_maker(docs, shard - lax.rem(shard, GROUP), rows)

    def tile(i, _):
        begin, allowed = masked(i)
        end = i + REACH + 1
        steps = (end - begin + WIDE - 1) // WIDE
        q = q_ref[rows_at(i, rows), :]
        g = g_ref[rows_at(i, rows), :]
        delta = d_ref[i, 0:1, :]
        logsum = l_ref[i, 0:1, :]

        def grads(c, dq):
            j = end - (c + 1) * WIDE
            at = wide_at(j, rows)
            k = k_ref[at, :]
            s = lax.dot_general(k, q, NT, preferred_element_type=jnp.float32)
            dprob = lax.dot_general(v_ref[at, :], g, NT, preferred_element_type=jnp.float32)
            prob = jnp.exp2(jnp.where(allowed(j), s * EXP2_SCALE - logsum, -1e30))
            ds = (prob * (dprob - delta)).astype(jnp.bfloat16)
            dv[at, :] += jnp.dot(prob.astype(jnp.bfloat16), g, preferred_element_type=jnp.float32)
            dk[at, :] += jnp.dot(ds, q, preferred_element_type=jnp.float32)
            return dq + lax.dot_general(ds, k, TN, preferred_element_type=jnp.float32)

        dq = lax.fori_loop(0, steps, grads, jnp.zeros((rows, DH), jnp.float32))
        dq_ref[rows_at(i, rows), :] = (dq * scale).astype(jnp.bfloat16)
        return 0

    lax.fori_loop(0, GROUP, tile, 0)
    halo = REACH * rows
    hk_ref[...] = (dk[:halo, :] * scale).astype(jnp.bfloat16)
    hv_ref[...] = dv[:halo, :].astype(jnp.bfloat16)
    dk_ref[...] = dk[halo:, :] * scale
    dv_ref[...] = dv[halo:, :]


def collect_kernel(
    dq_ref, dk_ref, dv_ref, hk_ref, hv_ref, qo, ko, vo, hk, hv, ks, vs, send, recv, hsend, hrecv, local
):
    rows = qo.shape[0]
    count, shard, device = place()
    me = lax.rem(shard, GROUP)
    base = shard - me
    ahead = device(lax.rem(shard + GROUP, count))
    behind = device(lax.rem(shard + count - GROUP, count))
    barrier = pltpu.get_barrier_semaphore()
    for j in range(1, GROUP):
        peer = device(base + lax.rem(me + j, GROUP))
        pl.semaphore_signal(barrier, inc=1, device_id=peer, device_id_type=MESH)
    pl.semaphore_signal(barrier, inc=1, device_id=ahead, device_id_type=MESH)
    pl.semaphore_wait(barrier, GROUP)

    halos = ((hk_ref, hk), (hv_ref, hv))

    def halo_copy(which, s):
        src, dst = halos[which]
        at = rows_at(s - 1, rows)
        return pltpu.make_async_remote_copy(
            src_ref=src.at[at, :],
            dst_ref=dst.at[at, :],
            send_sem=hsend.at[which, s],
            recv_sem=hrecv.at[which, s],
            device_id=behind,
            device_id_type=MESH,
        )

    tensors = ((dq_ref, qo), (ks, ko), (vs, vo))

    def out_copy(which, j):
        src, dst = tensors[which]
        peer = lax.rem(me + j, GROUP)
        return pltpu.make_async_remote_copy(
            src_ref=src.at[rows_at(peer, rows), :],
            dst_ref=dst.at[:, cols_at(me)],
            send_sem=send.at[which, j],
            recv_sem=recv.at[which, j],
            device_id=device(base + peer),
            device_id_type=MESH,
        )

    def in_copy(which, j):
        src, dst = tensors[which]
        peer = lax.rem(me + GROUP - j, GROUP)
        return pltpu.make_async_remote_copy(
            src_ref=src.at[rows_at(peer, rows), :],
            dst_ref=dst.at[:, cols_at(peer)],
            send_sem=send.at[which, j],
            recv_sem=recv.at[which, j],
            device_id=device(base + peer),
            device_id_type=MESH,
        )

    def own_copy(which):
        src, dst = tensors[which]
        return pltpu.make_async_copy(
            src.at[rows_at(me, rows), :], dst.at[:, cols_at(me)], local.at[which]
        )

    for j in range(GROUP):
        s = lax.rem(me + j, GROUP)

        @pl.when(s >= 1)
        def _():
            for which in range(2):
                halo_copy(which, s).start()

    own_copy(0).start()
    for j in range(1, GROUP):
        out_copy(0, j).start()

    for j in [*range(1, GROUP), 0]:
        s = lax.rem(me + j, GROUP)
        at = rows_at(s, rows)

        @pl.when(s == 0)
        def _():
            ks[at, :] = dk_ref[at, :].astype(jnp.bfloat16)
            vs[at, :] = dv_ref[at, :].astype(jnp.bfloat16)

        @pl.when(s >= 1)
        def _():
            before = rows_at(s - 1, rows)
            halo_copy(0, s).wait_recv()
            ks[at, :] = (dk_ref[at, :] + hk[before, :].astype(jnp.float32)).astype(jnp.bfloat16)
            halo_copy(1, s).wait_recv()
            vs[at, :] = (dv_ref[at, :] + hv[before, :].astype(jnp.float32)).astype(jnp.bfloat16)

        for which in (1, 2):
            if j:
                out_copy(which, j).start()
            else:
                own_copy(which).start()

    for which in range(3):
        own_copy(which).wait()
        for j in range(1, GROUP):
            in_copy(which, j).wait_recv()
    for which in range(3):
        for j in range(1, GROUP):
            out_copy(which, j).wait_send()
    for s in range(1, GROUP):
        for which in range(2):
            halo_copy(which, s).wait_send()


def per_device(query_rows, key_rows, value_rows, forward_out, out_grad, doc_blocks):
    rows, features = query_rows.shape
    bf16, f32 = jnp.bfloat16, jnp.float32
    own, window = GROUP * rows, (GROUP + REACH) * rows
    vmem = pl.BlockSpec(memory_space=pltpu.VMEM)
    dma = pltpu.SemaphoreType.DMA
    smem = pl.BlockSpec(memory_space=pltpu.SMEM)
    hbm = pl.BlockSpec(memory_space=pltpu.HBM)
    qh, gh, kw, vw, dh, lh = pl.pallas_call(
        spread_kernel,
        out_shape=(
            jax.ShapeDtypeStruct((own, DH), bf16),
            jax.ShapeDtypeStruct((own, DH), bf16),
            jax.ShapeDtypeStruct((window, DH), bf16),
            jax.ShapeDtypeStruct((window, DH), bf16),
            jax.ShapeDtypeStruct((GROUP, 8, rows), f32),
            jax.ShapeDtypeStruct((GROUP, 8, rows), f32),
        ),
        in_specs=[smem] + [hbm] * 5,
        out_specs=[vmem] * 6,
        scratch_shapes=[
            pltpu.VMEM((rows, features), bf16),
            pltpu.VMEM((rows, features), bf16),
            pltpu.VMEM((HEADS, 8, rows), f32),
            dma((5, GROUP)),
            dma((5, GROUP)),
            dma((2, GROUP)),
            dma((2, GROUP)),
            dma((7,)),
        ],
        compiler_params=pltpu.CompilerParams(
            collective_id=0, has_side_effects=True, vmem_limit_bytes=40 << 20
        ),
        name="spread",
    )(doc_blocks, query_rows, key_rows, value_rows, forward_out, out_grad)
    dq, dk, dv, hk, hv = pl.pallas_call(
        grad_kernel,
        out_shape=(
            jax.ShapeDtypeStruct((own, DH), bf16),
            jax.ShapeDtypeStruct((own, DH), f32),
            jax.ShapeDtypeStruct((own, DH), f32),
            jax.ShapeDtypeStruct((window - own, DH), bf16),
            jax.ShapeDtypeStruct((window - own, DH), bf16),
        ),
        in_specs=[smem] + [vmem] * 6,
        out_specs=[vmem] * 5,
        scratch_shapes=[
            pltpu.VMEM((window, DH), f32),
            pltpu.VMEM((window, DH), f32),
        ],
        compiler_params=pltpu.CompilerParams(vmem_limit_bytes=40 << 20),
        name="grad",
    )(doc_blocks, qh, gh, kw, vw, dh, lh)
    return pl.pallas_call(
        collect_kernel,
        out_shape=(jax.ShapeDtypeStruct((rows, features), bf16),) * 3,
        in_specs=[vmem] * 5,
        out_specs=[vmem] * 3,
        scratch_shapes=[
            pltpu.VMEM((window - own, DH), bf16),
            pltpu.VMEM((window - own, DH), bf16),
            pltpu.VMEM((own, DH), bf16),
            pltpu.VMEM((own, DH), bf16),
            dma((3, GROUP)),
            dma((3, GROUP)),
            dma((2, GROUP)),
            dma((2, GROUP)),
            dma((3,)),
        ],
        compiler_params=pltpu.CompilerParams(
            collective_id=1, has_side_effects=True, vmem_limit_bytes=40 << 20
        ),
        name="collect",
    )(dq, dk, dv, hk, hv)


def solution(mesh):
    rows = P(("cx", "cy"), None)
    return jax.shard_map(
        per_device,
        mesh=mesh,
        in_specs=(rows, rows, rows, rows, rows, P()),
        out_specs=(rows, rows, rows),
        check_vma=False,
    )
```

profile of v0, /device:TPU:9, one launch (start us, length us, event | category | flops | bytes accessed | tf_op | source)
XLA Modules:
  0.0 119.8 jit_solution(3828741615038782868)
XLA Ops:
  0.6 0.0 copy-start
  0.6 1.0 copy-done
  1.7 0.0 copy-start.1
  1.7 1.0 copy-done.1
  2.7 0.0 copy-start.2
  2.7 1.0 copy-done.2
  3.8 0.0 copy-start.3
  3.8 1.0 copy-done.3
  4.8 0.0 copy-start.4
  4.8 1.0 copy-done.4
  5.8 0.0 copy-start.5
  5.8 0.7 copy-done.5
  6.5 61.6 %spread.1 = (bf16[2048,128]{1,0:T(8,128)(2,1)S(1)}, bf16[2048,128]{1,0:T(8,128)(2,1)S(1)}, bf16[3840,128]{1,0:T(8,128)(2,1)S(1)}, bf16[3840,128]{1,0:T(8,128)(2,...) custom-call(s32[8]{0:T(128)S(1)} %copy-done.5, bf16[256,1024]{1,0:T(8,128)(2,1)S(1)} %copy-done, ...), custom_call_target="tpu_custom_call" | custom-call | tf_op jit(solution)/shard_map/spread/pallas_call | solution.py:405
  68.1 9.9 %grad.1 = (bf16[2048,128]{1,0:T(8,128)(2,1)S(1)}, f32[2048,128]{1,0:T(8,128)S(1)}, f32[2048,128]{1,0:T(8,128)S(1)}, bf16[1792,128]{1,0:T(8,128)(2,1)S(1)}, bf16[1792,128]{1,0:T(8,128)(2,1)S(1)}) custom-call(s32[8]{0:T(128)S(1)} %copy-done.5, bf16[2048,128]{1,0:T(8,128)(2,1)S(1)} %get-tuple-element.14.q_ref, bf16[2048,128]{1,0:T(8,128)(2,1)S(1)} %get-tuple-element.15.g_ref, ...), custom_call_target="tpu_custom_call" | custom-call | tf_op jit(solution)/shard_map/grad/pallas_call | solution.py:432
  78.1 39.3 %collect.1 = (bf16[256,1024]{1,0:T(8,128)(2,1)S(1)}, bf16[256,1024]{1,0:T(8,128)(2,1)S(1)}, bf16[256,1024]{1,0:T(8,128)(2,1)S(1)}) custom-call(bf16[2048,128]{1,0:T(8,128)(2,1)S(1)} %get-tuple-element.20.dq_ref, f32[2048,128]{1,0:T(8,128)S(1)} %get-tuple-element.21.dk_ref, f32[2048,128]{1,0:T(8,128)S(1)} %get-tuple-element.22.dv_ref, ...), custom_call_target="tpu_custom_call" | custom-call | tf_op jit(solution)/shard_map/collect/pallas_call | solution.py:450
  117.4 0.8 copy.12
  118.2 0.8 copy.13
  119.0 0.8 copy.14
Async XLA Ops:
  0.6 1.0 copy-start
  1.7 1.0 copy-start.1
  2.7 1.0 copy-start.2
  3.8 1.0 copy-start.3
  4.8 1.0 copy-start.4
  5.8 0.7 copy-start.5
where the time goes:
time: 122 us; the launch traced here: 120 us
  Pallas kernels  111 us (91%)
  local copies, waits for them, and re-layouts  8.23 us (7%)
    pallas_call x1, Pallas kernels, per_device(): pl.pallas_call(spread_kernel, out_shape=(jax.ShapeDtypeStruct((own, DH),...  61.6 us
    pallas_call x1, Pallas kernels, per_device(): pl.pallas_call(collect_kernel, out_shape=(jax.ShapeDtypeStruct((rows, fea...  39.3 us
    pallas_call x1, Pallas kernels, per_device(): pl.pallas_call(grad_kernel, out_shape=(jax.ShapeDtypeStruct((own, DH), bf...  9.95 us
    unnamed x15, local copies, waits for them, and re-layouts  8.23 us

commit v1 on v0

--- a/solution.py
+++ b/solution.py
@@ -120,7 +120,7 @@
     o_copy.start()
     pl.semaphore_wait(barrier, GROUP)
 
-    for which in (K, Q):
+    for which in (K, V):
         for j in range(1, GROUP):
             out_copy(which, j).start()
 
@@ -152,9 +152,11 @@
         delta_copy(j, lax.rem(me + j, GROUP), me).start()
 
     forward_all(K)
-    for which in (V, G):
-        for j in range(1, GROUP):
-            out_copy(which, j).start()
+    for j in range(1, GROUP):
+        out_copy(Q, j).start()
+    forward_all(V)
+    for j in range(1, GROUP):
+        out_copy(G, j).start()
     own_copy(Q).wait()
     for j in range(1, GROUP):
         in_copy(Q, j).wait_recv()
@@ -183,7 +185,6 @@
         return 0
 
     lax.fori_loop(0, GROUP, stats, 0)
-    forward_all(V)
     own_copy(G).wait()
     for j in range(1, GROUP):
         in_copy(G, j).wait_recv()

time: 122 us -> 118 us (0.967)
  Pallas kernels: 111 us -> 107 us
    pallas_call x1, Pallas kernels: 61.6 us -> 56.1 us  [per_device(): pl.pallas_call(spread_kernel, out_shape=(jax.ShapeDtypeStruct((own, DH),...]
    pallas_call x1, Pallas kernels: 39.3 us -> 42.2 us  [per_device(): pl.pallas_call(collect_kernel, out_shape=(jax.ShapeDtypeStruct((rows, fea...]
    pallas_call x1, Pallas kernels: 9.95 us -> 8.71 us  [per_device(): pl.pallas_call(grad_kernel, out_shape=(jax.ShapeDtypeStruct((own, DH), bf...]
where the time goes in v1:
time: 118 us; the launch traced here: 116 us
  Pallas kernels  107 us (91%)
  local copies, waits for them, and re-layouts  8.23 us (7%)
    pallas_call x1, Pallas kernels, per_device(): pl.pallas_call(spread_kernel, out_shape=(jax.ShapeDtypeStruct((own, DH),...  56.1 us
    pallas_call x1, Pallas kernels, per_device(): pl.pallas_call(collect_kernel, out_shape=(jax.ShapeDtypeStruct((rows, fea...  42.2 us
    pallas_call x1, Pallas kernels, per_device(): pl.pallas_call(grad_kernel, out_shape=(jax.ShapeDtypeStruct((own, DH), bf...  8.71 us
    unnamed x15, local copies, waits for them, and re-layouts  8.23 us

profile of v1, /device:TPU:9, one launch (start us, length us, event | category | flops | bytes accessed | tf_op | source)
XLA Modules:
  0.0 115.9 jit_solution(5364414492146430836)
XLA Ops:
  0.6 0.0 copy-start
  0.6 1.0 copy-done
  1.7 0.0 copy-start.1
  1.7 1.0 copy-done.1
  2.7 0.0 copy-start.2
  2.7 1.0 copy-done.2
  3.8 0.0 copy-start.3
  3.8 1.0 copy-done.3
  4.8 0.0 copy-start.4
  4.8 1.0 copy-done.4
  5.8 0.0 copy-start.5
  5.8 0.7 copy-done.5
  6.5 56.1 %spread.1 = (bf16[2048,128]{1,0:T(8,128)(2,1)S(1)}, bf16[2048,128]{1,0:T(8,128)(2,1)S(1)}, bf16[3840,128]{1,0:T(8,128)(2,1)S(1)}, bf16[3840,128]{1,0:T(8,128)(2,...) custom-call(s32[8]{0:T(128)S(1)} %copy-done.5, bf16[256,1024]{1,0:T(8,128)(2,1)S(1)} %copy-done, ...), custom_call_target="tpu_custom_call" | custom-call | tf_op jit(solution)/shard_map/spread/pallas_call | solution.py:406
  62.6 8.7 %grad.1 = (bf16[2048,128]{1,0:T(8,128)(2,1)S(1)}, f32[2048,128]{1,0:T(8,128)S(1)}, f32[2048,128]{1,0:T(8,128)S(1)}, bf16[1792,128]{1,0:T(8,128)(2,1)S(1)}, bf16[1792,128]{1,0:T(8,128)(2,1)S(1)}) custom-call(s32[8]{0:T(128)S(1)} %copy-done.5, bf16[2048,128]{1,0:T(8,128)(2,1)S(1)} %get-tuple-element.14.q_ref, bf16[2048,128]{1,0:T(8,128)(2,1)S(1)} %get-tuple-element.15.g_ref, ...), custom_call_target="tpu_custom_call" | custom-call | tf_op jit(solution)/shard_map/grad/pallas_call | solution.py:433
  71.3 42.2 %collect.1 = (bf16[256,1024]{1,0:T(8,128)(2,1)S(1)}, bf16[256,1024]{1,0:T(8,128)(2,1)S(1)}, bf16[256,1024]{1,0:T(8,128)(2,1)S(1)}) custom-call(bf16[2048,128]{1,0:T(8,128)(2,1)S(1)} %get-tuple-element.20.dq_ref, f32[2048,128]{1,0:T(8,128)S(1)} %get-tuple-element.21.dk_ref, f32[2048,128]{1,0:T(8,128)S(1)} %get-tuple-element.22.dv_ref, ...), custom_call_target="tpu_custom_call" | custom-call | tf_op jit(solution)/shard_map/collect/pallas_call | solution.py:451
  113.5 0.8 copy.12
  114.3 0.8 copy.13
  115.1 0.8 copy.14
Async XLA Ops:
  0.6 1.0 copy-start
  1.7 1.0 copy-start.1
  2.7 1.0 copy-start.2
  3.8 1.0 copy-start.3
  4.8 1.0 copy-start.4
  5.8 0.7 copy-start.5

commit v2 on v0

--- a/solution.py
+++ b/solution.py
@@ -92,20 +92,25 @@
             device_id_type=MESH,
         )
 
+    def forward_own(which):
+        own_copy(which).wait()
+
+        @pl.when(me >= 1)
+        def _():
+            forward(which, me).start()
+
+    def forward_from(which, j):
+        source = lax.rem(me + GROUP - j, GROUP)
+        in_copy(which, j).wait_recv()
+
+        @pl.when(source >= 1)
+        def _():
+            forward(which, source).start()
+
     def forward_all(which):
-        own_copy(which).wait()
-
-        @pl.when(me >= 1)
-        def _():
-            forward(which, me).start()
-
+        forward_own(which)
         for j in range(1, GROUP):
-            source = lax.rem(me + GROUP - j, GROUP)
-            in_copy(which, j).wait_recv()
-
-            @pl.when(source >= 1)
-            def _():
-                forward(which, source).start()
+            forward_from(which, j)
 
     g_copy = pltpu.make_async_copy(g_ref, g_here, local.at[5])
     o_copy = pltpu.make_async_copy(o_ref, o_here, local.at[6])
@@ -155,6 +160,7 @@
     for which in (V, G):
         for j in range(1, GROUP):
             out_copy(which, j).start()
+    forward_own(V)
     own_copy(Q).wait()
     for j in range(1, GROUP):
         in_copy(Q, j).wait_recv()
@@ -180,10 +186,14 @@
             )
             top = higher
         lh[i] = jnp.broadcast_to(top + jnp.log2(total), (8, rows))
+
+        @pl.when(i >= 1)
+        def _():
+            forward_from(V, i)
+
         return 0
 
     lax.fori_loop(0, GROUP, stats, 0)
-    forward_all(V)
     own_copy(G).wait()
     for j in range(1, GROUP):
         in_copy(G, j).wait_recv()

time: 122 us -> 115 us (0.943); the launches traced: 120 us -> 116 us
  Pallas kernels: 111 us -> 107 us
    pallas_call x1, Pallas kernels: 61.6 us -> 54.2 us  [per_device(): pl.pallas_call(spread_kernel, out_shape=(jax.ShapeDtypeStruct((own, DH),...]
    pallas_call x1, Pallas kernels: 9.95 us -> 14.3 us  [per_device(): pl.pallas_call(grad_kernel, out_shape=(jax.ShapeDtypeStruct((own, DH), bf...]
where the time goes in v2:
time: 115 us; the launch traced here: 116 us
  Pallas kernels  107 us (93%)
  local copies, waits for them, and re-layouts  8.23 us (7%)
    pallas_call x1, Pallas kernels, per_device(): pl.pallas_call(spread_kernel, out_shape=(jax.ShapeDtypeStruct((own, DH),...  54.2 us
    pallas_call x1, Pallas kernels, per_device(): pl.pallas_call(collect_kernel, out_shape=(jax.ShapeDtypeStruct((rows, fea...  38.3 us
    pallas_call x1, Pallas kernels, per_device(): pl.pallas_call(grad_kernel, out_shape=(jax.ShapeDtypeStruct((own, DH), bf...  14.3 us
    unnamed x15, local copies, waits for them, and re-layouts  8.23 us

profile of v2, /device:TPU:9, one launch (start us, length us, event | category | flops | bytes accessed | tf_op | source)
XLA Modules:
  0.0 115.7 jit_solution(2074993788890817368)
XLA Ops:
  0.6 0.0 copy-start
  0.6 1.0 copy-done
  1.7 0.0 copy-start.1
  1.7 1.0 copy-done.1
  2.7 0.0 copy-start.2
  2.7 1.0 copy-done.2
  3.8 0.0 copy-start.3
  3.8 1.0 copy-done.3
  4.8 0.0 copy-start.4
  4.8 1.0 copy-done.4
  5.8 0.0 copy-start.5
  5.8 0.7 copy-done.5
  6.5 54.2 %spread.1 = (bf16[2048,128]{1,0:T(8,128)(2,1)S(1)}, bf16[2048,128]{1,0:T(8,128)(2,1)S(1)}, bf16[3840,128]{1,0:T(8,128)(2,1)S(1)}, bf16[3840,128]{1,0:T(8,128)(2,...) custom-call(s32[8]{0:T(128)S(1)} %copy-done.5, bf16[256,1024]{1,0:T(8,128)(2,1)S(1)} %copy-done, ...), custom_call_target="tpu_custom_call" | custom-call | tf_op jit(solution)/shard_map/spread/pallas_call | solution.py:415
  60.7 14.3 %grad.1 = (bf16[2048,128]{1,0:T(8,128)(2,1)S(1)}, f32[2048,128]{1,0:T(8,128)S(1)}, f32[2048,128]{1,0:T(8,128)S(1)}, bf16[1792,128]{1,0:T(8,128)(2,1)S(1)}, bf16[1792,128]{1,0:T(8,128)(2,1)S(1)}) custom-call(s32[8]{0:T(128)S(1)} %copy-done.5, bf16[2048,128]{1,0:T(8,128)(2,1)S(1)} %get-tuple-element.14.q_ref, bf16[2048,128]{1,0:T(8,128)(2,1)S(1)} %get-tuple-element.15.g_ref, ...), custom_call_target="tpu_custom_call" | custom-call | tf_op jit(solution)/shard_map/grad/pallas_call | solution.py:442
  75.0 38.3 %collect.1 = (bf16[256,1024]{1,0:T(8,128)(2,1)S(1)}, bf16[256,1024]{1,0:T(8,128)(2,1)S(1)}, bf16[256,1024]{1,0:T(8,128)(2,1)S(1)}) custom-call(bf16[2048,128]{1,0:T(8,128)(2,1)S(1)} %get-tuple-element.20.dq_ref, f32[2048,128]{1,0:T(8,128)S(1)} %get-tuple-element.21.dk_ref, f32[2048,128]{1,0:T(8,128)S(1)} %get-tuple-element.22.dv_ref, ...), custom_call_target="tpu_custom_call" | custom-call | tf_op jit(solution)/shard_map/collect/pallas_call | solution.py:460
  113.3 0.8 copy.12
  114.1 0.8 copy.13
  114.9 0.8 copy.14
Async XLA Ops:
  0.6 1.0 copy-start
  1.7 1.0 copy-start.1
  2.7 1.0 copy-start.2
  3.8 1.0 copy-start.3
  4.8 1.0 copy-start.4
  5.8 0.7 copy-start.5

commit v3 on v2

--- a/solution.py
+++ b/solution.py
@@ -435,7 +435,7 @@
             dma((7,)),
         ],
         compiler_params=pltpu.CompilerParams(
-            collective_id=0, has_side_effects=True, vmem_limit_bytes=40 << 20
+            collective_id=0, has_side_effects=True, vmem_limit_bytes=60 << 20
         ),
         name="spread",
     )(doc_blocks, query_rows, key_rows, value_rows, forward_out, out_grad)
@@ -454,7 +454,7 @@
             pltpu.VMEM((window, DH), f32),
             pltpu.VMEM((window, DH), f32),
         ],
-        compiler_params=pltpu.CompilerParams(vmem_limit_bytes=40 << 20),
+        compiler_params=pltpu.CompilerParams(vmem_limit_bytes=60 << 20),
         name="grad",
     )(doc_blocks, qh, gh, kw, vw, dh, lh)
     return pl.pallas_call(
@@ -474,7 +474,7 @@
             dma((3,)),
         ],
         compiler_params=pltpu.CompilerParams(
-            collective_id=1, has_side_effects=True, vmem_limit_bytes=40 << 20
+            collective_id=1, has_side_effects=True, vmem_limit_bytes=60 << 20
         ),
         name="collect",
     )(dq, dk, dv, hk, hv)

time: 115 us -> 118 us (1.026)
  Pallas kernels: 107 us -> 113 us
  local copies, waits for them, and re-layouts: 8.23 us -> 3.95 us
    pallas_call x1, Pallas kernels: 38.3 us -> 45.3 us  [per_device(): pl.pallas_call(collect_kernel, out_shape=(jax.ShapeDtypeStruct((rows, fea...]
    unnamed x15 -> x7, local copies, waits for them, and re-layouts: 8.23 us -> 3.95 us
    pallas_call x1, Pallas kernels: 14.3 us -> 11.7 us  [per_device(): pl.pallas_call(grad_kernel, out_shape=(jax.ShapeDtypeStruct((own, DH), bf...]
    pallas_call x1, Pallas kernels: 54.2 us -> 56.1 us  [per_device(): pl.pallas_call(spread_kernel, out_shape=(jax.ShapeDtypeStruct((own, DH),...]
where the time goes in v3:
time: 118 us
  Pallas kernels  113 us (96%)
  local copies, waits for them, and re-layouts  3.95 us (3%)
    pallas_call x1, Pallas kernels, per_device(): pl.pallas_call(spread_kernel, out_shape=(jax.ShapeDtypeStruct((own, DH),...  56.1 us
    pallas_call x1, Pallas kernels, per_device(): pl.pallas_call(collect_kernel, out_shape=(jax.ShapeDtypeStruct((rows, fea...  45.3 us
    pallas_call x1, Pallas kernels, per_device(): pl.pallas_call(grad_kernel, out_shape=(jax.ShapeDtypeStruct((own, DH), bf...  11.7 us
    unnamed x7, local copies, waits for them, and re-layouts  3.95 us

profile of v3, /device:TPU:9, one launch (start us, length us, event | category | flops | bytes accessed | tf_op | source)
XLA Modules:
  0.0 117.7 jit_solution(17130785154508096509)
XLA Ops:
  0.6 56.1 %spread.1 = (bf16[2048,128]{1,0:T(8,128)(2,1)}, bf16[2048,128]{1,0:T(8,128)(2,1)}, bf16[3840,128]{1,0:T(8,128)(2,1)}, bf16[3840,128]{1,0:T(8,128)(2,1)}, f32[8,8,256]{2,1,0:T(8,128)}, /*index=5*/f32[8,8,256]{2,1,0:T(8,128)}) custom-call(s32[8]{0:T(128)} %docs.3, bf16[256,1024]{1,0:T(8,128)(2,1)} %q_ref.1, bf16[256,1024]{1,0:T(8,128)(2,1)} %k_ref.1, ...), custom_call_target="tpu_custom_call" | custom-call | tf_op jit(solution)/shard_map/spread/pallas_call | solution.py:415
  56.8 11.7 %grad.1 = (bf16[2048,128]{1,0:T(8,128)(2,1)}, f32[2048,128]{1,0:T(8,128)}, f32[2048,128]{1,0:T(8,128)}, bf16[1792,128]{1,0:T(8,128)(2,1)}, bf16[1792,128]{1,0:T(8,128)(2,1)}) custom-call(s32[8]{0:T(128)} %docs.3, bf16[2048,128]{1,0:T(8,128)(2,1)} %get-tuple-element.14.q_ref, bf16[2048,128]{1,0:T(8,128)(2,1)} %get-tuple-element.15.g_ref, ...), custom_call_target="tpu_custom_call" | custom-call | tf_op jit(solution)/shard_map/grad/pallas_call | solution.py:442
  68.5 45.3 %collect.1 = (bf16[256,1024]{1,0:T(8,128)(2,1)}, bf16[256,1024]{1,0:T(8,128)(2,1)}, bf16[256,1024]{1,0:T(8,128)(2,1)}) custom-call(bf16[2048,128]{1,0:T(8,128)(2,1)} %get-tuple-element.20.dq_ref, f32[2048,128]{1,0:T(8,128)} %get-tuple-element.21.dk_ref, f32[2048,128]{1,0:T(8,128)} %get-tuple-element.22.dv_ref, bf16[1792,128]{1,0:T(8,128)(2,1)} %get-tuple-element.23.hk_ref, ...), custom_call_target="tpu_custom_call" | custom-call | tf_op jit(solution)/shard_map/collect/pallas_call | solution.py:460
  113.8 0.0 copy-start.1
  113.8 1.9 %copy.12 = bf16[256,1024]{1,0:T(8,128)(2,1)} copy(bf16[256,1024]{1,0:T(8,128)(2,1)} %get-tuple-element.28) | data formatting | bytes 1048576
  115.7 0.0 copy-done.1
  115.7 0.0 copy-start
  115.7 0.8 copy.13
  116.5 0.4 copy-done
  116.9 0.8 copy.14
Async XLA Ops:
  113.8 1.9 %copy-start.1 = (bf16[256,1024]{1,0:T(8,128)(2,1)S(1)}, bf16[256,1024]{1,0:T(8,128)(2,1)}, u32[]{:S(2)}) copy-start(bf16[256,1024]{1,0:T(8,128)(2,1)} %get-tuple-element.29) | copy-start | bytes 1572868
  115.7 1.2 %copy-start = (bf16[256,1024]{1,0:T(8,128)(2,1)S(1)}, bf16[256,1024]{1,0:T(8,128)(2,1)}, u32[]{:S(2)}) copy-start(bf16[256,1024]{1,0:T(8,128)(2,1)} %get-tuple-element.30) | copy-start | bytes 1572868
